TPU v7x, 32 devices: a whole 2x2x4 slice. The times are simulated.
32 devices in a mesh: row: 8 (over z, core), col: 4 (over y, x).
Axes of the slice: x: 2, y: 2, z: 4, core: 2. Of those that a mesh axis runs over, the one named last changes fastest.
Arguments:
- gbar: float32 [16, 1024, 32, 512], P(None, 'row', None, 'col'), as said below
- panel: float32 [32, 512, 256], P(None, ('col', 'row')), may hold values from -0.046875 to 0.046875
- panel_adj: float32 [16, 1024, 256], P(None, ('row', 'col')), may hold values from -6 to 6
- factor: float32 [256, 256], replicated, as said below
- factor_adj: float32 [256, 256], replicated, may hold values from -6 to 6
Outputs:
- lower_adj: float32 [16, 1024, 256], P(None, ('row', 'col'))
- corner_adj: float32 [256, 256], replicated
Inputs may be any that keep to these rules, and one draw needn't show every extreme that they name: gbar holds a symmetric 16384 x 16384 matrix. factor is lower triangular with a positive diagonal.
All inputs are finite; a program needn't handle non-finite values.
Results may differ from a plain program's by a relative error of at most 0.000075.
Values sent between devices are 32-bit elements; how exact they have to be, the bound alone decides.
A program may use at most 128 MiB of HBM per device.

v0:
```python
import jax
import jax.numpy as jnp
from jax import lax
from jax.sharding import PartitionSpec as P


def broadcast(value, axis, source):
    kept = jnp.where(lax.axis_index(axis) == source, value, 0).astype(value.dtype)
    return lax.psum(kept, axis)


def corner_reduce(corner):
    return lax.psum(corner, ("row", "col"))


def per_device(gbar, panel, panel_adj, factor, factor_adj):
    highest = lax.Precision.HIGHEST
    row_at = lax.axis_index("row")
    col_at = lax.axis_index("col")
    n_row = lax.axis_size("row")
    n_col = lax.axis_size("col")
    panel_width = factor.shape[0]
    row_share = panel_adj.shape[1]
    column = lax.all_gather(panel, "row", axis=1, tiled=True)
    product = jnp.einsum(
        "arcs,csk->ark", gbar, column, precision=highest, preferred_element_type=jnp.float32
    )
    spread = jnp.zeros(product.shape, jnp.float32)
    spread = lax.dynamic_update_slice_in_dim(spread, panel_adj, col_at * row_share, 1)
    partial_value = spread - 2.0 * product
    inverse = jax.scipy.linalg.solve_triangular(
        factor, jnp.eye(panel_width, dtype=jnp.float32), lower=True
    )
    stride_ratio = n_row // n_col
    blocks = column.shape[0] // stride_ratio
    local_rows = lax.dynamic_index_in_dim(
        column.reshape(blocks, stride_ratio, column.shape[1], panel_width),
        row_at // n_col,
        1,
        keepdims=False,
    )
    rows_here = broadcast(local_rows, "col", row_at % n_col)
    mine = lax.dynamic_slice_in_dim(rows_here, col_at * row_share, row_share, 1)
    summed = lax.psum(partial_value, "col")
    owned_part = lax.dynamic_slice_in_dim(summed, col_at * row_share, row_share, 1)
    owned_rows = jnp.einsum(
        "ark,kj->arj", owned_part, inverse, precision=highest, preferred_element_type=jnp.float32
    )
    corner = jnp.einsum(
        "ark,arj->kj", owned_rows, mine, precision=highest, preferred_element_type=jnp.float32
    )
    corner_total = corner_reduce(corner)
    adjusted = factor_adj - corner_total
    projected = jnp.dot(factor.T, adjusted, precision=highest, preferred_element_type=jnp.float32)
    halved = jnp.tril(projected) - 0.5 * jnp.diag(jnp.diag(projected))
    middle = jnp.dot(
        jnp.dot(inverse.T, halved, precision=highest, preferred_element_type=jnp.float32),
        inverse,
        precision=highest,
        preferred_element_type=jnp.float32,
    )
    return (owned_rows, 0.5 * (middle + middle.T))


def solution(mesh):
    return jax.shard_map(
        per_device,
        mesh=mesh,
        in_specs=(
            P(None, "row", None, "col"),
            P(None, ("col", "row"), None),
            P(None, ("row", "col"), None),
            P(),
            P(),
        ),
        out_specs=(P(None, ("row", "col"), None), P()),
        check_vma=False,
    )
```

profile of v0, /device:TPU:0, one launch (start us, length us, event | category | flops | bytes accessed | tf_op | source)
XLA Modules:
  0.0 361.2 jit_solution(14952034391698706143)
XLA Ops:
  7.2 0.0 all-gather.2.cloned.1.call-start
  7.2 0.7 all-gather.2.cloned.1.call-update
  7.9 0.0 all-reduce.6.cloned.1.call-start
  8.0 0.2 broadcast_in_dim.31
  8.3 51.2 %all-gather.2.cloned.1.call-done = f32[32,128,256]{2,1,0:T(8,128)} async-done(((f32[32,16,256]{2,1,0:T(8,128)}), f32[32,128,256]{2,1,0:T(8,128)}) %all-gather.2.cloned.1.call-update) | async-done | bytes 4194320 | tf_op jit(solution)/shard_map/all_gather | solution.py:24
  59.5 3.3 select_bitcast_fusion
  62.8 50.8 %fusion.3 = f32[16,128,256]{2,1,0:T(8,128)} fusion(f32[16,128,256]{2,1,0:T(8,128)S(1)} %constant_dynamic-update-slice_fusion, f32[32,128,256]{2,1,0:T(8,128)S(1)} %copy-done, f32[16,128,32,128]{3,2,1,0:T(8,128)} %param.5), kind=kOutput, calls=%fused_computation.7 | convolution fusion | flops 25770852352 | bytes 41943040 | tf_op jit(solution)/shard_map/arcs,csk->ark/dot_general | solution.py:25
  113.6 0.0 all-reduce.4.cloned.1.call-start
  113.7 0.9 copy-done.1
  114.6 0.1 copy.11
  114.7 0.1 triangular_solve.68
  114.8 4.3 %while.1 = (s32[]{:T(128)}, f32[256,256]{0,1:T(8,128)S(1)}, s32[2,2]{1,0:T(2,128)S(1)}, f32[2,128,128]{2,1,0:T(8,128)S(1)}, s32[]{:T(128)}) while((s32[]{:T(128)}, f32[256,256]{0,1:T(8,128)S(1)}, s32[2,2]{1,0:T(2,128)S(1)}, f32[2,128,128]{2,1,0:T(8,128)S(1)}, s32[]{:T(128)}) %tuple.27), condition=%wide.while_cond, body=%wide.while_body.sunk | while | flops 2 | bytes 393329 | solution.py:31
  114.8 0.6 fusion.42
  115.4 1.4 dynamic-slice.7
  116.8 0.1 copy.23
  117.0 0.6 fusion.42
  117.6 1.4 dynamic-slice.7
  119.0 0.1 copy.23
  119.1 19.7 %custom-call.4 = f32[2,128,128]{1,2,0:T(8,128)S(1)} custom-call(f32[2,128,128]{2,1,0:T(8,128)S(1)} %get-tuple-element.9), custom_call_target="InvertDiagBlocksLowerTriangular" | custom-call | tf_op jit(solution)/shard_map/jit(_solve_triangular)/triangular_solve | solution.py:31
  138.8 0.3 fusion.24
  139.1 0.4 convolution_subtract_fusion
  139.5 0.3 fusion.27
  139.8 76.9 %all-reduce.6.cloned.1.call-done = (f32[16,128,256]{2,1,0:T(8,128)}, f32[16,128,256]{2,1,0:T(8,128)}) async-done(((f32[16,128,256]{2,1,0:T(8,128)}, f32[16,128,256]{2,1,0:T(8,128)}), (f32[16,128,256]{2,1,0:T(8,128)}, f32[16,128,256]{2,1,0:T(8,128)})) %all-reduce.6.cloned.1.call-update) | async-done | bytes 4194320 | tf_op jit(solution)/shard_map/psum | solution.py:44
  216.7 1.6 fusion.9
  218.4 3.0 convolution_bitcast_fusion.1
  221.3 127.4 %all-reduce.4.cloned.1.call-done = f32[256,256]{1,0:T(8,128)} async-done(((f32[256,256]{1,0:T(8,128)}), f32[256,256]{1,0:T(8,128)}) %all-reduce.4.cloned.1.call-update) | async-done | bytes 262160 | tf_op jit(solution)/shard_map/psum | solution.py:13
  348.7 1.5 convolution_bitcast_fusion
  350.3 2.4 gather_fusion
  352.7 0.6 fusion.13
  353.3 0.4 fusion.20
  353.7 0.1 copy.13
  353.8 0.8 copy.14
  (22 shorter events, 0.3 us)
Async XLA Ops:
  7.2 1.0 copy-start.3
  7.2 52.3 %all-gather.2.cloned.1.call-start = ((), (), s32[]{:S(2)}) async-start(), calls=%async_computation | async-start | bytes 4718592 | tf_op jit(solution)/shard_map/all_gather | solution.py:24
  7.9 208.8 %all-reduce.6.cloned.1.call-start = ((), (), s32[]{:S(2)}) async-start(), calls=%async_computation.2 | async-start | bytes 8388608 | tf_op jit(solution)/shard_map/psum | solution.py:44
  59.5 3.3 copy-start
  113.6 0.9 copy-start.1
  113.6 235.1 %all-reduce.4.cloned.1.call-start = ((), (), s32[]{:S(2)}) async-start(), calls=%async_computation.1 | async-start | bytes 524288 | tf_op jit(solution)/shard_map/psum | solution.py:13
  139.1 209.6 %copy-start.4 = (f32[256,256]{1,0:T(8,128)S(1)}, f32[256,256]{1,0:T(8,128)}, u32[]{:S(2)}) copy-start(f32[256,256]{1,0:T(8,128)} %param.9) | copy-start | bytes 786436
  218.3 134.3 %copy-start.2 = (f32[16,32,256]{2,1,0:T(8,128)}, f32[16,32,256]{2,1,0:T(8,128)S(1)}, u32[]{:S(2)}) copy-start(f32[16,32,256]{2,1,0:T(8,128)S(1)} %fusion.9) | copy-start | bytes 1572868
Sparse Core Ops, SparseCore 0:
  9.6 49.8 all-gather.1
  113.7 102.9 all-reduce.5
  223.7 124.9 all-reduce.3
where the time goes:
time: 362 us; the launch traced here: 361 us
  waiting for transfers between devices  256 us (71%)
  matrix products  58.9 us (16%)
  other arithmetic  23 us (6%)
  between operations  14 us (4%)
  local copies, waits for them, and re-layouts  8.94 us (2%)
    psum x1, waiting for transfers between devices, corner_reduce(): return lax.psum(corner, ('row', 'col'))  127 us
    psum x1, waiting for transfers between devices, per_device(): summed = lax.psum(partial_value, 'col')  76.9 us
    all_gather x1, waiting for transfers between devices, per_device(): column = lax.all_gather(panel, 'row', axis=1, tiled=True)  51.2 us
    dot_general x1, matrix products, per_device(): jnp.einsum('arcs,csk->ark', gbar, column, precision=highest, preferred_el...  50.8 us
    another operation x3, other arithmetic, per_device(): jax.scipy.linalg.solve_triangular(factor, jnp.eye(panel_width, dtype=jnp....  19.7 us
  transfers between devices with their start and end apart: 3, of which 3 were waited for; matrix products, arithmetic and copies ran while one was open for 7% of the time, Pallas kernels for 0%

commit v1 on v0

--- a/solution.py
+++ b/solution.py
@@ -1,6 +1,10 @@
+import functools
+
 import jax
 import jax.numpy as jnp
 from jax import lax
+from jax.experimental import pallas as pl
+from jax.experimental.pallas import tpu as pltpu
 from jax.sharding import PartitionSpec as P
 
 
@@ -13,7 +17,7 @@
     return lax.psum(corner, ("row", "col"))
 
 
-def per_device(gbar, panel, panel_adj, factor, factor_adj):
+def plain_device(gbar, panel, panel_adj, factor, factor_adj):
     highest = lax.Precision.HIGHEST
     row_at = lax.axis_index("row")
     col_at = lax.axis_index("col")
@@ -60,6 +64,406 @@
         preferred_element_type=jnp.float32,
     )
     return (owned_rows, 0.5 * (middle + middle.T))
+
+
+HALVES = 2
+PARTS = 2
+TILES = 4
+BASE = 32
+MESH = pl.DeviceIdType.MESH
+
+
+def exact(a, b, dims=((1,), (0,))):
+    return lax.dot_general(
+        a,
+        b,
+        (dims, ((), ())),
+        precision=lax.Precision.HIGHEST,
+        preferred_element_type=jnp.float32,
+    )
+
+
+def lower_inverse(factor):
+    n = factor.shape[0]
+    groups = n // BASE
+    rows = lax.broadcasted_iota(jnp.int32, (n, n), 0)
+    cols = lax.broadcasted_iota(jnp.int32, (n, n), 1)
+    factor = jnp.where(rows >= cols, factor, 0.0)
+    same = (rows // BASE) == (cols // BASE)
+    at_row = lax.broadcasted_iota(jnp.int32, (n, 128), 0)
+    at_col = lax.broadcasted_iota(jnp.int32, (n, 128), 1)
+    pick = jnp.where(at_row % BASE == at_col, 1.0, 0.0).astype(jnp.float32)
+    compact = exact(jnp.where(same, factor, 0.0), pick).reshape(groups, BASE, 128)
+    solved = pick.reshape(groups, BASE, 128)
+    inner = lax.broadcasted_iota(jnp.int32, (groups, BASE, 128), 1)
+    for j in range(BASE):
+        line = solved[:, j : j + 1, :] / compact[:, j : j + 1, j : j + 1]
+        below = compact[:, :, j : j + 1] * line
+        solved = jnp.where(inner == j, line, jnp.where(inner > j, solved - below, solved))
+    full = jnp.where(same, exact(solved.reshape(n, 128), pick, ((1,), (1,))), 0.0)
+    size = BASE
+    while size < n:
+        off = ((rows // (2 * size)) == (cols // (2 * size))) & ((rows // size) > (cols // size))
+        cross = exact(exact(full, jnp.where(off, factor, 0.0)), full)
+        full = full - cross
+        size *= 2
+    return full
+
+
+def fused(
+    n_row, n_col,
+    gbar, panel, panel_adj, factor, factor_adj,
+    owned_out, corner_out,
+    stage, high, low, gathered, right, acc, parts_in, mine, inverse_ref, part, mids, mid, smalls, total,
+    stage_sem, own_sem, z_send, z_recv, sib_send, sib_recv, fwd_send, fwd_recv,
+    rs_send, rs_recv, mine_send, mine_recv, a_send, a_recv, b_send, b_recv, c_send, c_recv, d_send, d_recv,
+):
+    row = lax.axis_index("row")
+    col = lax.axis_index("col")
+    nz = n_row // 2
+    z = row // 2
+    core = row % 2
+    blocks, height = panel_adj.shape[0], panel_adj.shape[1]
+    groups = 2 * panel.shape[0]
+    share = panel.shape[2]
+    width = factor.shape[0]
+    half_width = width // HALVES
+    per_part = groups // PARTS
+    tall = n_col * height
+    depth = n_row * share
+
+    def z_row(d, c):
+        return lax.rem(z + d + nz, nz) * 2 + c
+
+    sibling = z * 2 + 1 - core
+
+    def load(b, slot):
+        return pltpu.make_async_copy(gbar.at[b], stage.at[slot], stage_sem.at[slot])
+
+    load(0, 0).start()
+    load(1, 1).start()
+
+    items = [(h, j) for h in range(HALVES) for j in range(PARTS)]
+
+    def slot_of(q, source):
+        h, j = items[q]
+        half = per_part // 2
+        return gathered.at[h, pl.ds(j * half, half), :, source]
+
+    def remote(src, dst, ssem, rsem, r, c):
+        return pltpu.make_async_remote_copy(
+            src_ref=src, dst_ref=dst, send_sem=ssem, recv_sem=rsem, device_id=(r, c), device_id_type=MESH
+        )
+
+    def flat(h, j):
+        half = per_part // 2
+        return panel.at[pl.ds(j * half, half), :, :, pl.ds(h * half_width, half_width)]
+
+    def z_copy(q, d):
+        return remote(flat(*items[q]), slot_of(q, row), z_send.at[q, d - 1], z_recv.at[q, d - 1], z_row(d, core), col)
+
+    def sib_copy(q):
+        return remote(flat(*items[q]), slot_of(q, row), sib_send.at[q], sib_recv.at[q], sibling, col)
+
+    def fwd_copy(q, d):
+        source = z_row(-d, core)
+        return remote(
+            slot_of(q, source), slot_of(q, source), fwd_send.at[q, d - 1], fwd_recv.at[q, d - 1], sibling, col
+        )
+
+    def own_copy(q):
+        return pltpu.make_async_copy(flat(*items[q]), slot_of(q, row), own_sem.at[q])
+
+    for q in range(len(items)):
+        for d in range(1, nz):
+            z_copy(q, d).start()
+        sib_copy(q).start()
+        own_copy(q).start()
+
+    def prepare(pair, carry):
+        for slot in range(2):
+            b = pair * 2 + slot
+            load(b, slot).wait()
+            for c in range(groups):
+                value = stage[slot, pl.ds(c, tall, stride=groups), :]
+                top = value.astype(jnp.bfloat16)
+                rest = (value - top.astype(jnp.float32)).astype(jnp.bfloat16)
+                at = pl.ds(pl.multiple_of(b * tall, tall), tall)
+                high[at, c * depth : (c + 1) * depth] = top
+                low[at, c * depth : (c + 1) * depth] = rest
+
+            @pl.when(b + 2 < blocks)
+            def _():
+                load(b + 2, slot).start()
+
+        return carry
+
+    lax.fori_loop(0, blocks // 2, prepare, 0)
+    inverse_ref[...] = lower_inverse(factor[...])
+
+    tile_blocks = blocks // TILES
+    tile_rows = tile_blocks * tall
+
+    def rs_copy(h, d, m):
+        peer = lax.rem(col + d, n_col)
+        at = pl.ds(m * tile_blocks, tile_blocks)
+        return remote(
+            acc.at[h, at, pl.ds(pl.multiple_of(peer * height, height), height)],
+            parts_in.at[d - 1, h, at],
+            rs_send.at[h, d - 1, m],
+            rs_recv.at[h, d - 1, m],
+            row,
+            peer,
+        )
+
+    def compute(q):
+        h, j = items[q]
+        own_copy(q).wait()
+        sib_copy(q).wait_recv()
+        for d in range(1, nz):
+            fwd_copy(q, d).wait_recv()
+        values = gathered[h, j * per_part // 2 : (j + 1) * per_part // 2].reshape(per_part * depth, half_width)
+        top = values.astype(jnp.bfloat16)
+        right[:, :half_width] = top
+        right[:, half_width:] = (values - top.astype(jnp.float32)).astype(jnp.bfloat16)
+
+        def tile(m, carry):
+            at = pl.ds(pl.multiple_of(m * tile_rows, tile_rows), tile_rows)
+            span = pl.ds(j * per_part * depth, per_part * depth)
+            both = jnp.dot(high[at, span], right[...], preferred_element_type=jnp.float32)
+            small = jnp.dot(low[at, span], right[:, :half_width], preferred_element_type=jnp.float32)
+            out = (both[:, :half_width] + (both[:, half_width:] + small)).reshape(tile_blocks, tall, half_width)
+            where = pl.ds(m * tile_blocks, tile_blocks)
+            if j == 0:
+                acc[h, where] = out
+            else:
+                acc[h, where] += out
+            if j == PARTS - 1:
+                for d in range(1, n_col):
+                    rs_copy(h, d, m).start()
+            return carry
+
+        lax.fori_loop(0, TILES, tile, 0)
+
+    to_half = lax.rem(row, 2)
+
+    def mine_dst():
+        return mine.at[:, pl.ds(pl.multiple_of(to_half * share, share), share)]
+
+    def mine_copy(p):
+        return remote(panel.at[:, p], mine_dst(), mine_send.at[p], mine_recv.at[to_half], col + p * n_col, row // 2)
+
+    def is_self(p):
+        return (col + p * n_col == row) & (row // 2 == col)
+
+    def mine_start(p):
+        @pl.when(is_self(p))
+        def _():
+            pltpu.make_async_copy(panel.at[:, p], mine_dst(), mine_recv.at[to_half]).start()
+
+        @pl.when(jnp.logical_not(is_self(p)))
+        def _():
+            mine_copy(p).start()
+
+    for q in range(len(items) + 1):
+        if q < len(items):
+            for d in range(1, nz):
+                z_copy(q, d).wait_recv()
+                fwd_copy(q, d).start()
+        if q == len(items) - 1:
+            mine_start(0)
+            mine_start(1)
+        if q >= 1:
+            compute(q - 1)
+
+    at_mine = pl.ds(pl.multiple_of(col * height, height), height)
+    pieces = []
+    for h in range(HALVES):
+        for d in range(1, n_col):
+            for m in range(TILES):
+                rs_copy(h, d, m).wait_recv()
+        summed = acc[h, :, at_mine, :]
+        for d in range(1, n_col):
+            summed = summed + parts_in[d - 1, h]
+        lanes = slice(h * half_width, (h + 1) * half_width)
+        pieces.append((panel_adj[:, :, lanes] - 2.0 * summed).reshape(blocks * height, half_width))
+    inverse = inverse_ref[...]
+    owned = exact(jnp.concatenate(pieces, axis=1), inverse)
+    owned_out[...] = owned.reshape(blocks, height, width)
+    for p in range(2):
+        pltpu.make_async_copy(
+            panel.at[:, p], mine.at[:, pl.ds(p * share, share)], mine_recv.at[p]
+        ).wait()
+    part[...] = exact(owned.T, mine[...].reshape(blocks * height, width))
+
+    big = width // n_col
+    tiny = big // n_row
+
+    def a_copy(d):
+        peer = lax.rem(col + d, n_col)
+        src = part.at[pl.ds(pl.multiple_of(peer * big, big), big)]
+        return remote(src, mids.at[d - 1], a_send.at[d - 1], a_recv.at[d - 1], row, peer)
+
+    def b_copy(d):
+        peer = lax.rem(row + d, n_row)
+        src = mid.at[pl.ds(pl.multiple_of(peer * tiny, tiny), tiny)]
+        return remote(src, smalls.at[d - 1], b_send.at[d - 1], b_recv.at[d - 1], peer, col)
+
+    def c_ref(r):
+        return total.at[pl.ds(pl.multiple_of(col * big + r * tiny, tiny), tiny)]
+
+    def c_copy(d):
+        return remote(c_ref(row), c_ref(row), c_send.at[d - 1], c_recv.at[d - 1], lax.rem(row + d, n_row), col)
+
+    def c_from(d):
+        src = c_ref(lax.rem(row - d + n_row, n_row))
+        return remote(src, src, c_send.at[d - 1], c_recv.at[d - 1], lax.rem(row + d, n_row), col)
+
+    def d_ref(c):
+        return total.at[pl.ds(pl.multiple_of(c * big, big), big)]
+
+    def d_copy(d):
+        return remote(d_ref(col), d_ref(col), d_send.at[d - 1], d_recv.at[d - 1], row, lax.rem(col + d, n_col))
+
+    def d_from(d):
+        src = d_ref(lax.rem(col - d + n_col, n_col))
+        return remote(src, src, d_send.at[d - 1], d_recv.at[d - 1], row, lax.rem(col + d, n_col))
+
+    for d in range(1, n_col):
+        a_copy(d).start()
+    summed = part[pl.ds(pl.multiple_of(col * big, big), big), :]
+    for d in range(1, n_col):
+        a_copy(d).wait_recv()
+        summed = summed + mids[d - 1]
+    mid[...] = summed
+    for d in range(1, n_row):
+        b_copy(d).start()
+    summed = mid[pl.ds(pl.multiple_of(row * tiny, tiny), tiny), :]
+    for d in range(1, n_row):
+        b_copy(d).wait_recv()
+        summed = summed + smalls[d - 1]
+    total[pl.ds(pl.multiple_of(col * big + row * tiny, tiny), tiny), :] = summed
+    for d in range(1, n_row):
+        c_copy(d).start()
+    for d in range(1, n_row):
+        c_from(d).wait_recv()
+    for d in range(1, n_col):
+        d_copy(d).start()
+    for d in range(1, n_col):
+        d_from(d).wait_recv()
+
+    adjusted = factor_adj[...] - total[...]
+    projected = exact(factor[...].T, adjusted)
+    rows = lax.broadcasted_iota(jnp.int32, (width, width), 0)
+    cols = lax.broadcasted_iota(jnp.int32, (width, width), 1)
+    halved = jnp.where(rows > cols, projected, jnp.where(rows == cols, 0.5 * projected, 0.0))
+    middle = exact(exact(inverse.T, halved), inverse)
+    corner_out[...] = 0.5 * (middle + middle.T)
+
+    for q in range(len(items)):
+        for d in range(1, nz):
+            z_copy(q, d).wait_send()
+            fwd_copy(q, d).wait_send()
+        sib_copy(q).wait_send()
+    for h in range(HALVES):
+        for d in range(1, n_col):
+            for m in range(TILES):
+                rs_copy(h, d, m).wait_send()
+    for p in range(2):
+        @pl.when(jnp.logical_not(is_self(p)))
+        def _(p=p):
+            mine_copy(p).wait_send()
+    for d in range(1, n_col):
+        a_copy(d).wait_send()
+        d_copy(d).wait_send()
+    for d in range(1, n_row):
+        b_copy(d).wait_send()
+        c_copy(d).wait_send()
+
+
+def fast_device(n_row, n_col, gbar, panel, panel_adj, factor, factor_adj):
+    blocks, tall, groups, depth = gbar.shape
+    share, width = panel.shape[1], panel.shape[2]
+    height = panel_adj.shape[1]
+    half_width = width // HALVES
+    nz = n_row // 2
+    items = HALVES * PARTS
+    f32, bf16 = jnp.float32, jnp.bfloat16
+    dma = pltpu.SemaphoreType.DMA
+    vmem = pl.BlockSpec(memory_space=pltpu.VMEM)
+    return pl.pallas_call(
+        functools.partial(fused, n_row, n_col),
+        out_shape=(
+            jax.ShapeDtypeStruct(panel_adj.shape, f32),
+            jax.ShapeDtypeStruct(factor.shape, f32),
+        ),
+        in_specs=[pl.BlockSpec(memory_space=pl.ANY)] + [vmem] * 4,
+        out_specs=(vmem, vmem),
+        scratch_shapes=[
+            pltpu.VMEM((2, tall * groups, depth), f32),
+            pltpu.VMEM((blocks * tall, groups * depth), bf16),
+            pltpu.VMEM((blocks * tall, groups * depth), bf16),
+            pltpu.VMEM((HALVES, groups // 2, 2, n_row, share, half_width), f32),
+            pltpu.VMEM((groups // PARTS * depth, width), bf16),
+            pltpu.VMEM((HALVES, blocks, tall, half_width), f32),
+            pltpu.VMEM((n_col - 1, HALVES, blocks, height, half_width), f32),
+            pltpu.VMEM((blocks, height, width), f32),
+            pltpu.VMEM((width, width), f32),
+            pltpu.VMEM((width, width), f32),
+            pltpu.VMEM((n_col - 1, width // n_col, width), f32),
+            pltpu.VMEM((width // n_col, width), f32),
+            pltpu.VMEM((n_row - 1, width // n_col // n_row, width), f32),
+            pltpu.VMEM((width, width), f32),
+            dma((2,)),
+            dma((items,)),
+            dma((items, nz - 1)),
+            dma((items, nz - 1)),
+            dma((items,)),
+            dma((items,)),
+            dma((items, nz - 1)),
+            dma((items, nz - 1)),
+            dma((HALVES, n_col - 1, TILES)),
+            dma((HALVES, n_col - 1, TILES)),
+            dma((2,)),
+            dma((2,)),
+            dma((n_col - 1,)),
+            dma((n_col - 1,)),
+            dma((n_row - 1,)),
+            dma((n_row - 1,)),
+            dma((n_row - 1,)),
+            dma((n_row - 1,)),
+            dma((n_col - 1,)),
+            dma((n_col - 1,)),
+        ],
+        compiler_params=pltpu.CompilerParams(
+            has_side_effects=True, vmem_limit_bytes=60 * 1024 * 1024
+        ),
+    )(
+        gbar.reshape(blocks, tall * groups, depth),
+        panel.reshape(groups // 2, 2, share, width),
+        panel_adj,
+        factor,
+        factor_adj,
+    )
+
+
+def per_device(gbar, panel, panel_adj, factor, factor_adj):
+    n_row, n_col = lax.axis_size("row"), lax.axis_size("col")
+    width = factor.shape[0]
+    blocks, tall, groups, depth = gbar.shape
+    fits = (
+        n_row == 2 * n_col
+        and groups == 2 * blocks
+        and panel.shape[1] % 8 == 0
+        and depth == 128
+        and width == 256
+        and blocks % TILES == 0
+        and width % (8 * n_row * n_col) == 0
+        and gbar.size * 4 <= 36 * 1024 * 1024
+    )
+    if fits:
+        return fast_device(n_row, n_col, gbar, panel, panel_adj, factor, factor_adj)
+    return plain_device(gbar, panel, panel_adj, factor, factor_adj)
 
 
 def solution(mesh):

time: 362 us -> 120 us (0.33)
  waiting for transfers between devices: 256 us -> 0 us
  Pallas kernels: 0 us -> 116 us
  matrix products: 58.9 us -> 0 us
  other arithmetic: 23 us -> 0 us
  between operations: 14 us -> 0.64 us
  local copies, waits for them, and re-layouts: 8.94 us -> 3.55 us
    psum x2 -> x0, waiting for transfers between devices: 204 us -> none  [the longest x1 127 us: corner_reduce(): return lax.psum(corner, ('row', 'col'))]
    pallas_call x0 -> x1, Pallas kernels: none -> 116 us  [fast_device(): pl.pallas_call(functools.partial(fused, n_row, n_col), out_shape=(jax.Sha...]
    dot_general x6 -> x0, matrix products: 57.9 us -> none  [the longest x1 50.8 us: per_device(): jnp.einsum('arcs,csk->ark', gbar, column, precision=highest, preferred_el...]
    all_gather x1 -> x0, waiting for transfers between devices: 51.2 us -> none  [per_device(): column = lax.all_gather(panel, 'row', axis=1, tiled=True)]
    another operation x3 -> x0, other arithmetic: 19.7 us -> none  [per_device(): jax.scipy.linalg.solve_triangular(factor, jnp.eye(panel_width, dtype=jnp....]
    another operation x11 -> x0, local copies, waits for them, and re-layouts: 4.33 us -> none
  transfers between devices with their start and end apart: 3 -> 0, of which waited for: 3 -> 0; matrix products, arithmetic and copies ran while one was open for 7% -> 0% of each run, Pallas kernels for 0% -> 0%
where the time goes in v1:
time: 120 us
  Pallas kernels  116 us (97%)
  local copies, waits for them, and re-layouts  3.55 us (3%)
    pallas_call x1, Pallas kernels, fast_device(): pl.pallas_call(functools.partial(fused, n_row, n_col), out_shape=(jax.Sha...  116 us
    unnamed x2, local copies, waits for them, and re-layouts  3.55 us

profile of v1, /device:TPU:0, one launch (start us, length us, event | category | flops | bytes accessed | tf_op | source)
XLA Modules:
  0.0 120.1 jit_solution(4808863369141539136)
XLA Ops:
  0.6 115.9 %shard_map.68 = (f32[16,32,256]{2,1,0:T(8,128)}, f32[256,256]{1,0:T(8,128)}) custom-call(f32[16,4096,128]{2,1,0:T(8,128)} %bitcast.2, f32[16,2,16,256]{3,2,1,0:T(8,128)} %bitcast.3, f32[16,32,256]{2,1,0:T(8,128)} %panel_adj.1, f32[256,256]{1,0:T(8,128)} %factor.1, f32[256,256]{1,0:T(8,128)} %factor_adj.1), custom_call_target="tpu_custom_call" | custom-call | tf_op jit(solution)/shard_map/pallas_call | solution.py:394
  116.5 1.9 %copy.9 = f32[16,32,256]{2,1,0:T(8,128)} copy(f32[16,32,256]{2,1,0:T(8,128)} %get-tuple-element.4) | data formatting | bytes 1048576
  118.4 1.7 %copy.10 = f32[256,256]{1,0:T(8,128)} copy(f32[256,256]{1,0:T(8,128)} %get-tuple-element.5) | data formatting | bytes 524288
